TPU v7x, 32 devices: a whole 2x2x4 slice. The times are simulated.
32 devices in a mesh: rep: 4 (over y, core), fsdp: 8 (over z, x).
Axes of the slice: x: 2, y: 2, z: 4, core: 2. Of those that a mesh axis runs over, the one named last changes fastest.
Arguments:
- tokens: bfloat16 [8192, 8192], P(('rep', 'fsdp')), may hold values from -6 to 6
- cotangent: bfloat16 [8192, 512], P(('rep', 'fsdp')), may hold values from -0.29882812 to 0.29882812
- anchor: float32 [8192, 512], P('fsdp'), may hold values from -0.0625 to 0.0625
- momentum: float32 [8192, 512], P('fsdp'), may hold values from -0.02 to 0.02
- first_moment: float32 [4, 8192, 512], P('rep', 'fsdp'), may hold values from -2 to 2
- second_moment: float32 [4, 8192, 512], P('rep', 'fsdp'), may hold values from 0.05 to 1
- inner_offset: float32 [4, 8192, 512], P('rep', 'fsdp'), may hold values from -0.03 to 0.03
Outputs:
- keys: bfloat16 [8192, 512], P(('rep', 'fsdp'))
- first_new: float32 [4, 8192, 512], P('rep', 'fsdp')
- second_new: float32 [4, 8192, 512], P('rep', 'fsdp')
All inputs are finite; a program needn't handle non-finite values.
Results may differ from a plain program's by a relative error of at most 0.005.
Values may be sent and summed in bfloat16 or wider, within the bound.
A program may use at most 128 MiB of HBM per device.

v0:
```python
import jax
import jax.numpy as jnp
from jax import lax
from jax.sharding import PartitionSpec as P


def contract_rows(left, right):
    return lax.dot_general(
        left, right, (((0,), (0,)), ((), ())), preferred_element_type=jnp.float32
    )


def outer_step(pseudo, anchor, momentum):
    momentum_new = 0.9 * momentum + pseudo
    anchor_new = anchor - 0.7 * (pseudo + 0.9 * momentum_new)
    return anchor_new.astype(jnp.bfloat16)


def on_device(tokens, cotangent, anchor, momentum, first_moment, second_moment, inner_offset):
    selected = tokens
    grad = lax.psum_scatter(
        contract_rows(selected, cotangent), "fsdp", scatter_dimension=0, tiled=True
    )
    grad = grad[None]
    first_new = 0.9 * first_moment + 0.1 * grad
    second_new = 0.95 * second_moment + 0.05 * grad * grad
    current = anchor[None] + inner_offset
    inner = current - 0.001 * (first_new / (jnp.sqrt(second_new) + 1e-08) + 0.1 * current)
    delta = anchor - inner[0]
    groups = lax.axis_size("rep")
    pseudo = lax.psum(delta, "rep") / groups
    weights = outer_step(pseudo, anchor, momentum)
    selected = tokens
    keys = jnp.dot(
        selected,
        lax.all_gather(weights, "fsdp", axis=0, tiled=True),
        preferred_element_type=jnp.float32,
    )
    return (keys.astype(jnp.bfloat16), first_new, second_new)


def solution(mesh):
    return jax.shard_map(
        on_device,
        mesh=mesh,
        in_specs=(
            P(("rep", "fsdp"), None),
            P(("rep", "fsdp"), None),
            P("fsdp", None),
            P("fsdp", None),
            P("rep", "fsdp", None),
            P("rep", "fsdp", None),
            P("rep", "fsdp", None),
        ),
        out_specs=(P(("rep", "fsdp"), None), P("rep", "fsdp", None), P("rep", "fsdp", None)),
        check_vma=False,
    )
```

profile of v0, /device:TPU:17, one launch (start us, length us, event | category | flops | bytes accessed | tf_op | source)
XLA Modules:
  0.0 502.1 jit_solution(1633005389802902546)
XLA Ops:
  7.2 0.0 copy-start
  7.2 0.0 reduce-scatter.2.cloned.1.call-start
  7.2 0.9 copy-done
  8.1 10.3 %fusion.4 = f32[8192,512]{1,0:T(8,128)} fusion(bf16[256,8192]{1,0:T(8,128)(2,1)} %param.7, bf16[256,512]{1,0:T(8,128)(2,1)S(1)} %copy-done), kind=kOutput, calls=%fused_computation.9 | convolution fusion | flops 2147483648 | bytes 21233664 | tf_op jit(solution)/shard_map/dot_general | solution.py:8
  18.4 0.0 copy-start.1
  18.4 0.0 reduce-scatter.2.cloned.1.call-update
  18.4 0.0 all-reduce.2.cloned.1.call-start
  18.5 282.2 %reduce-scatter.2.cloned.1.call-done = f32[1024,512]{1,0:T(8,128)} async-done(((f32[8192,512]{1,0:T(8,128)}), f32[1024,512]{1,0:T(8,128)}) %reduce-scatter.2.cloned.1.call-update) | async-done | bytes 2097168 | tf_op jit(solution)/shard_map/reduce_scatter | solution.py:21
  300.7 0.0 copy-done.1
  300.7 7.3 %bitcast_subtract_fusion = (f32[1024,512]{1,0:T(8,128)}, f32[1,1024,512]{2,1,0:T(8,128)}, f32[1,1024,512]{2,1,0:T(8,128)}) fusion(f32[1024,512]{1,0:T(8,128)S(1)} %copy-done.1, f32[1,1024,512]{2,1,0:T(8,128)} %param.13, f32[1024,512]{1,0:T(8,128)} %reduce-scatter.2.cloned.1.call-done, f32[1,1024,512]{2,1,0:T(8,128)} %param.12, f32[1,1024,512]{2,1,0:T(8,128)} %param.11), kind=kLoop, calls=%fused_computation.3 | loop fusion | flops 7864320 | bytes 16777216 | tf_op jit(solution)/shard_map/sub | solution.py:29
  308.0 0.0 all-reduce.2.cloned.1.call-update
  308.0 0.0 all-gather.2.cloned.1.call-start
  308.1 51.7 %all-reduce.2.cloned.1.call-done = f32[1024,512]{1,0:T(8,128)} async-done(((f32[1024,512]{1,0:T(8,128)}), f32[1024,512]{1,0:T(8,128)}) %all-reduce.2.cloned.1.call-update) | async-done | bytes 2097168 | tf_op jit(solution)/shard_map/psum | solution.py:31
  359.8 4.1 subtract_convert_fusion
  363.9 0.0 all-gather.2.cloned.1.call-update
  363.9 123.9 %all-gather.2.cloned.1.call-done = bf16[8192,512]{1,0:T(8,128)(2,1)} async-done(((bf16[1024,512]{1,0:T(8,128)(2,1)}), bf16[8192,512]{1,0:T(8,128)(2,1)}) %all-gather.2.cloned.1.call-update) | async-done | bytes 8388624 | tf_op jit(solution)/shard_map/all_gather | solution.py:36
  487.8 6.9 %fusion.2 = bf16[256,512]{0,1:T(8,128)(2,1)S(1)} fusion(bf16[8192,512]{1,0:T(8,128)(2,1)} %all-gather.2.cloned.1.call-done, bf16[256,8192]{1,0:T(8,128)(2,1)} %param.7), kind=kOutput, calls=%fused_computation.8 | convolution fusion | flops 2147614720 | bytes 12845056 | tf_op jit(solution)/shard_map/dot_general | solution.py:34
  494.8 0.8 copy.10
Async XLA Ops:
  7.2 1.0 copy-start
  7.2 293.6 %reduce-scatter.2.cloned.1.call-start = ((), (), s32[]{:S(2)}) async-start(), calls=%async_computation.1 | async-start | bytes 18874368 | tf_op jit(solution)/shard_map/reduce_scatter | solution.py:21
  18.4 282.3 %copy-start.1 = (f32[1024,512]{1,0:T(8,128)S(1)}, f32[1024,512]{1,0:T(8,128)}, u32[]{:S(2)}) copy-start(f32[1024,512]{1,0:T(8,128)} %param.9) | copy-start | bytes 6291460
  18.4 341.3 %all-reduce.2.cloned.1.call-start = ((), (), s32[]{:S(2)}) async-start(), calls=%async_computation.2 | async-start | bytes 4194304 | tf_op jit(solution)/shard_map/psum | solution.py:31
  308.0 179.8 %all-gather.2.cloned.1.call-start = ((), (), s32[]{:S(2)}) async-start(), calls=%async_computation.3 | async-start | bytes 9437184 | tf_op jit(solution)/shard_map/all_gather | solution.py:36
Sparse Core Ops, SparseCore 0:
  18.6 282.1 reduce-scatter.1
  308.2 51.5 all-reduce.1
  364.0 123.7 all-gather.1
where the time goes:
time: 505 us; the launch traced here: 502 us
  waiting for transfers between devices  458 us (91%)
  matrix products  17.2 us (3%)
  between operations  13.8 us (3%)
  other arithmetic  11.4 us (2%)
    reduce_scatter x1, waiting for transfers between devices, on_device(): lax.psum_scatter(contract_rows(selected, cotangent), 'fsdp', scatter_dime...  282 us
    all_gather x1, waiting for transfers between devices, on_device(): lax.all_gather(weights, 'fsdp', axis=0, tiled=True)  124 us
    psum x1, waiting for transfers between devices, on_device(): pseudo = lax.psum(delta, 'rep') / groups  51.7 us
    dot_general x1, matrix products, contract_rows(): lax.dot_general(left, right, (((0,), (0,)), ((), ())), preferred_element_...  10.3 us
  transfers between devices with their start and end apart: 3, of which 3 were waited for; matrix products, arithmetic and copies ran while one was open for 0% of the time, Pallas kernels for 0%

commit v1 on v0

v1 whole, which is shorter than its diff:
```python
import functools
import jax
import jax.numpy as jnp
from jax import lax
from jax.experimental import pallas as pl
from jax.experimental.pallas import tpu as pltpu
from jax.sharding import PartitionSpec as P

VMEM = pl.BlockSpec(memory_space=pltpu.VMEM)


def remote(src, dst, send_sem, recv_sem, rep, fsdp):
    return pltpu.make_async_remote_copy(
        src_ref=src,
        dst_ref=dst,
        send_sem=send_sem,
        recv_sem=recv_sem,
        device_id=(rep, fsdp),
        device_id_type=pl.DeviceIdType.MESH,
    )


def greet(rep, fsdp):
    pl.semaphore_signal(
        pltpu.get_barrier_semaphore(),
        inc=1,
        device_id=(rep, fsdp),
        device_id_type=pl.DeviceIdType.MESH,
    )


def contract_rows(left, right):
    return lax.dot_general(
        left, right, (((0,), (0,)), ((), ())), preferred_element_type=jnp.float32
    )


def grad_kernel(
    n, tokens, cot, grad, tok_p, cot_p, part, recv,
    cot_send, cot_recv, tok_send, tok_recv, part_send, part_recv,
):
    outer = n // 2
    rows = grad.shape[0]
    tile = min(rows, 256)
    r, f = lax.axis_index("rep"), lax.axis_index("fsdp")
    o, b = f // 2, f % 2
    partner = 2 * o + 1 - b

    greet(r, partner)

    @pl.loop(1, outer)
    def _(k):
        greet(r, 2 * ((o + k) % outer) + b)

    pl.semaphore_wait(pltpu.get_barrier_semaphore(), outer)

    def cot_copy():
        return remote(cot, cot_p, cot_send, cot_recv, r, partner)

    def tok_copy(k):
        col = pl.multiple_of((2 * ((o + k) % outer) + 1 - b) * rows, rows)
        return remote(
            tokens.at[:, pl.ds(col, rows)], tok_p.at[k],
            tok_send.at[k], tok_recv.at[k], r, partner,
        )

    def part_copy(k):
        return remote(
            part.at[k], recv.at[k], part_send.at[k], part_recv.at[k],
            r, 2 * ((o + k) % outer) + b,
        )

    def partial(k, j):
        first = pl.multiple_of(j * tile, tile)
        col = pl.multiple_of((2 * ((o + k) % outer) + b) * rows + first, tile)
        return contract_rows(tokens[:, pl.ds(col, tile)], cot[...]) + contract_rows(
            tok_p[k, :, pl.ds(first, tile)], cot_p[...]
        )

    cot_copy().start()

    @pl.loop(1, outer)
    def _(k):
        tok_copy(k).start()

    tok_copy(0).start()
    cot_copy().wait_recv()

    @pl.loop(1, outer)
    def _(k):
        tok_copy(k).wait_recv()

        @pl.loop(0, rows // tile)
        def _(j):
            at = pl.ds(pl.multiple_of(j * tile, tile), tile)
            part[k, at, :] = partial(k, j).astype(part.dtype)

        part_copy(k).start()

    tok_copy(0).wait_recv()

    @pl.loop(0, rows // tile)
    def _(j):
        grad[pl.ds(pl.multiple_of(j * tile, tile), tile), :] = partial(0, j)

    @pl.loop(1, outer)
    def _(k):
        part_copy(k).wait_recv()

        @pl.loop(0, rows // tile)
        def _(j):
            at = pl.ds(pl.multiple_of(j * tile, tile), tile)
            grad[at, :] += recv[k, at, :].astype(jnp.float32)

    cot_copy().wait_send()
    tok_copy(0).wait_send()

    @pl.loop(1, outer)
    def _(k):
        tok_copy(k).wait_send()
        part_copy(k).wait_send()


def group_grad(mesh, tokens, cotangent):
    n = mesh.shape["fsdp"]
    outer = n // 2
    count, width = tokens.shape
    kh = cotangent.shape[1]
    rows = width // n
    dma = pltpu.SemaphoreType.DMA
    return pl.pallas_call(
        functools.partial(grad_kernel, n),
        out_shape=jax.ShapeDtypeStruct((rows, kh), jnp.float32),
        in_specs=[VMEM] * 2,
        out_specs=VMEM,
        scratch_shapes=[
            pltpu.VMEM((outer, count, rows), jnp.bfloat16),
            pltpu.VMEM((count, kh), jnp.bfloat16),
            pltpu.VMEM((outer, rows, kh), jnp.bfloat16),
            pltpu.VMEM((outer, rows, kh), jnp.bfloat16),
            dma, dma, dma((outer,)), dma((outer,)), dma((outer,)), dma((outer,)),
        ],
        compiler_params=pltpu.CompilerParams(
            collective_id=0, has_side_effects=True, vmem_limit_bytes=40 * 2**20
        ),
    )(tokens, cotangent)


def keys_kernel(
    n, tokens, delta, anchor, momentum, keys, got, weights, total,
    got_send, got_recv, z_send, z_recv, x_send, x_recv,
    y_send, y_recv, c_send, c_recv, d_send, d_recv,
):
    outer = n // 2
    rows = anchor.shape[0]
    quarter = rows // 4
    r, f = lax.axis_index("rep"), lax.axis_index("fsdp")
    o, b = f // 2, f % 2
    partner = 2 * o + 1 - b
    over, near = (r + 2) % 4, r + 1 - 2 * (r % 2)

    greet(r, partner)

    @pl.loop(1, outer)
    def _(k):
        greet(r, 2 * ((o + k) % outer) + b)

    for m in range(1, 4):
        greet((r + m) % 4, f)
    pl.semaphore_wait(pltpu.get_barrier_semaphore(), outer + 3)

    def quarter_of(rep):
        return pl.ds(pl.multiple_of(rep * quarter, quarter), quarter)

    def chunk(fsdp, rep):
        return weights.at[pl.ds(pl.multiple_of(fsdp * rows + rep * quarter, quarter), quarter)]

    def got_copy(m):
        to = (r + m) % 4
        return remote(
            delta.at[quarter_of(to)], got.at[m - 1],
            got_send.at[m - 1], got_recv.at[m - 1], to, f,
        )

    for m in (2, 1, 3):
        got_copy(m).start()
    mine = quarter_of(r)
    for m in (1, 2, 3):
        got_copy(m).wait_recv()
    pseudo = (
        (delta[mine, :].astype(jnp.float32) + got[0].astype(jnp.float32))
        + (got[1].astype(jnp.float32) + got[2].astype(jnp.float32))
    ) / 4
    momentum_new = 0.9 * momentum[mine, :] + pseudo
    anchor_new = anchor[mine, :] - 0.7 * (pseudo + 0.9 * momentum_new)
    own = pl.ds(pl.multiple_of(f * rows + r * quarter, quarter), quarter)
    weights[own, :] = anchor_new.astype(weights.dtype)

    def z_copy(k):
        ref = chunk(f, r)
        return remote(ref, ref, z_send.at[k], z_recv.at[k], r, 2 * ((o + k) % outer) + b)

    def source(k, parity):
        return 2 * ((o + outer - k) % outer) + parity

    def x_copy(k):
        ref = chunk(source(k, b), r)
        return remote(ref, ref, x_send.at[k], x_recv.at[k], r, partner)

    def y_copy(k, s):
        ref = chunk(source(k, b if s == 0 else 1 - b), r)
        return remote(ref, ref, y_send.at[k, s], y_recv.at[k, s], over, f)

    def c_copy(k, s):
        ref = chunk(source(k, b if s == 0 else 1 - b), r)
        return remote(ref, ref, c_send.at[k, s], c_recv.at[k, s], near, f)

    def d_copy(k, s):
        ref = chunk(source(k, b if s == 0 else 1 - b), over)
        return remote(ref, ref, d_send.at[k, s], d_recv.at[k, s], near, f)

    @pl.loop(1, outer)
    def _(k):
        z_copy(k).start()

    total[...] = jnp.zeros_like(total)

    @pl.loop(0, outer + 3)
    def _(i):
        @pl.when(i < outer)
        def _():
            @pl.when(i > 0)
            def _():
                z_copy(i).wait_recv()

            x_copy(i).start()
            y_copy(i, 0).start()
            c_copy(i, 0).start()

        @pl.when((i >= 1) & (i < outer + 1))
        def _():
            x_copy(i - 1).wait_recv()
            y_copy(i - 1, 1).start()
            c_copy(i - 1, 1).start()

        @pl.when((i >= 2) & (i < outer + 2))
        def _():
            for s in range(2):
                y_copy(i - 2, s).wait_recv()
                d_copy(i - 2, s).start()

        @pl.when(i >= 3)
        def _():
            k = i - 3
            for s in range(2):
                c_copy(k, s).wait_recv()
                d_copy(k, s).wait_recv()
            at = pl.ds(pl.multiple_of(source(k, 0) * rows, 2 * rows), 2 * rows)
            total[...] += jnp.dot(
                tokens[:, at], weights[at, :], preferred_element_type=jnp.float32
            )

    keys[...] = total[...].astype(keys.dtype)
    for m in (1, 2, 3):
        got_copy(m).wait_send()

    @pl.loop(0, outer)
    def _(k):
        @pl.when(k > 0)
        def _():
            z_copy(k).wait_send()

        x_copy(k).wait_send()
        for s in range(2):
            y_copy(k, s).wait_send()
            c_copy(k, s).wait_send()
            d_copy(k, s).wait_send()


def keys_of(mesh, tokens, delta, anchor, momentum):
    n = mesh.shape["fsdp"]
    outer = n // 2
    count, width = tokens.shape
    rows, kh = anchor.shape
    dma = pltpu.SemaphoreType.DMA
    return pl.pallas_call(
        functools.partial(keys_kernel, n),
        out_shape=jax.ShapeDtypeStruct((count, kh), jnp.bfloat16),
        in_specs=[VMEM] * 4,
        out_specs=VMEM,
        scratch_shapes=[
            pltpu.VMEM((3, rows // 4, kh), jnp.bfloat16),
            pltpu.VMEM((width, kh), jnp.bfloat16),
            pltpu.VMEM((count, kh), jnp.float32),
            dma((3,)), dma((3,)),
            dma((outer,)), dma((outer,)), dma((outer,)), dma((outer,)),
            dma((outer, 2)), dma((outer, 2)), dma((outer, 2)), dma((outer, 2)),
            dma((outer, 2)), dma((outer, 2)),
        ],
        compiler_params=pltpu.CompilerParams(
            collective_id=1, has_side_effects=True, vmem_limit_bytes=40 * 2**20
        ),
    )(tokens, delta, anchor, momentum)


def on_device(mesh, tokens, cotangent, anchor, momentum, first_moment, second_moment, inner_offset):
    grad = group_grad(mesh, tokens, cotangent)[None]
    first_new = 0.9 * first_moment + 0.1 * grad
    second_new = 0.95 * second_moment + 0.05 * grad * grad
    current = anchor[None] + inner_offset
    inner = current - 0.001 * (first_new / (jnp.sqrt(second_new) + 1e-08) + 0.1 * current)
    delta = (anchor - inner[0]).astype(jnp.bfloat16)
    keys = keys_of(mesh, tokens, delta, anchor, momentum)
    return (keys, first_new, second_new)


def solution(mesh):
    return jax.shard_map(
        functools.partial(on_device, mesh),
        mesh=mesh,
        in_specs=(
            P(("rep", "fsdp"), None),
            P(("rep", "fsdp"), None),
            P("fsdp", None),
            P("fsdp", None),
            P("rep", "fsdp", None),
            P("rep", "fsdp", None),
            P("rep", "fsdp", None),
        ),
        out_specs=(P(("rep", "fsdp"), None), P("rep", "fsdp", None), P("rep", "fsdp", None)),
        check_vma=False,
    )
```

time: 505 us -> 201 us (0.40)
  waiting for transfers between devices: 458 us -> 0 us
  Pallas kernels: 0 us -> 189 us
  matrix products: 17.2 us -> 0 us
  between operations: 13.8 us -> 0.69 us
  other arithmetic: 11.4 us -> 5.35 us
    reduce_scatter x1 -> x0, waiting for transfers between devices: 282 us -> none  [on_device(): lax.psum_scatter(contract_rows(selected, cotangent), 'fsdp', scatter_dime...]
    pallas_call x0 -> x2, Pallas kernels: none -> 189 us  [the longest x1 111 us: group_grad(): pl.pallas_call(functools.partial(grad_kernel, n), out_shape=jax.ShapeDtyp...]
    all_gather x1 -> x0, waiting for transfers between devices: 124 us -> none  [on_device(): lax.all_gather(weights, 'fsdp', axis=0, tiled=True)]
    psum x1 -> x0, waiting for transfers between devices: 51.7 us -> none  [on_device(): pseudo = lax.psum(delta, 'rep') / groups]
    dot_general x2 -> x0, matrix products: 17.2 us -> none  [the longest x1 10.3 us: contract_rows(): lax.dot_general(left, right, (((0,), (0,)), ((), ())), preferred_element_...]
    sub x1 -> x0, other arithmetic: 7.28 us -> none  [on_device(): delta = anchor - inner[0]]
  transfers between devices with their start and end apart: 3 -> 0, of which waited for: 3 -> 0; matrix products, arithmetic and copies ran while one was open for 0% -> 0% of each run, Pallas kernels for 0% -> 0%
where the time goes in v1:
time: 201 us; the launch traced here: 198 us
  Pallas kernels  189 us (94%)
  other arithmetic  5.35 us (3%)
  local copies, waits for them, and re-layouts  3.85 us (2%)
    pallas_call x1, Pallas kernels, group_grad(): pl.pallas_call(functools.partial(grad_kernel, n), out_shape=jax.ShapeDtyp...  111 us
    pallas_call x1, Pallas kernels, keys_of(): pl.pallas_call(functools.partial(keys_kernel, n), out_shape=jax.ShapeDtyp...  77.3 us
    convert_element_type x1, other arithmetic, on_device(): delta = (anchor - inner[0]).astype(jnp.bfloat16)  5.35 us

profile of v1, /device:TPU:17, one launch (start us, length us, event | category | flops | bytes accessed | tf_op | source)
XLA Modules:
  0.0 198.5 jit_solution(13635828185969265316)
XLA Ops:
  0.6 0.0 copy-start
  0.6 2.2 %copy-done = bf16[256,8192]{1,0:T(8,128)(2,1)S(1)} copy-done((bf16[256,8192]{1,0:T(8,128)(2,1)S(1)}, bf16[256,8192]{1,0:T(8,128)(2,1)}, u32[]{:S(2)}) %copy-start) | copy-done | bytes 4194328
  2.8 0.0 copy-start.3
  2.8 0.9 copy-done.3
  3.8 0.0 copy-start.1
  3.8 0.0 copy-start.4
  3.8 0.0 copy-start.5
  3.8 111.3 %shard_map.94 = f32[1024,512]{1,0:T(8,128)S(1)} custom-call(bf16[256,8192]{1,0:T(8,128)(2,1)S(1)} %copy-done, bf16[256,512]{1,0:T(8,128)(2,1)S(1)} %copy-done.3), custom_call_target="tpu_custom_call" | custom-call | tf_op jit(solution)/shard_map/pallas_call | solution.py:131
  115.1 0.0 copy-done.1
  115.1 0.0 copy-done.4
  115.1 0.0 copy-done.5
  115.1 0.0 copy-start.2
  115.1 5.3 %fusion.2 = (bf16[1024,512]{1,0:T(8,128)(2,1)S(1)}, f32[1,1024,512]{2,1,0:T(8,128)}, f32[1,1024,512]{2,1,0:T(8,128)}) fusion(f32[1024,512]{1,0:T(8,128)S(1)} %copy-done.1, f32[1,1024,512]{2,1,0:T(8,128)S(1)} %copy-done.4, f32[1024,512]{1,0:T(8,128)S(1)} %shard_map.94, f32[1,1024,512]{2,1,0:T(8,128)S(1)} %copy-done.5, f32[1,1024,512]{2,1,0:T(8,128)} %param.11), kind=kLoop, calls=%fused_computation.4 | loop fusion | flops 8388608 | bytes 15728640 | tf_op jit(solution)/shard_map/convert_element_type | solution.py:312
  120.4 0.0 copy-done.2
  120.5 77.3 %shard_map.95 = bf16[256,512]{1,0:T(8,128)(2,1)S(1)} custom-call(bf16[256,8192]{1,0:T(8,128)(2,1)S(1)} %copy-done, bf16[1024,512]{1,0:T(8,128)(2,1)S(1)} %get-tuple-element.3.delta, f32[1024,512]{1,0:T(8,128)S(1)} %copy-done.1, f32[1024,512]{1,0:T(8,128)S(1)} %copy-done.2), custom_call_target="tpu_custom_call" | custom-call | tf_op jit(solution)/shard_map/pallas_call | solution.py:286
  197.8 0.7 copy.11
Async XLA Ops:
  0.6 2.2 %copy-start = (bf16[256,8192]{1,0:T(8,128)(2,1)S(1)}, bf16[256,8192]{1,0:T(8,128)(2,1)}, u32[]{:S(2)}) copy-start(bf16[256,8192]{1,0:T(8,128)(2,1)} %tokens.3) | copy-start | bytes 12582916
  2.8 0.9 copy-start.3
  3.8 111.3 %copy-start.1 = (f32[1024,512]{1,0:T(8,128)S(1)}, f32[1024,512]{1,0:T(8,128)}, u32[]{:S(2)}) copy-start(f32[1024,512]{1,0:T(8,128)} %anchor.1) | copy-start | bytes 6291460
  3.8 111.3 %copy-start.4 = (f32[1,1024,512]{2,1,0:T(8,128)S(1)}, f32[1,1024,512]{2,1,0:T(8,128)}, u32[]{:S(2)}) copy-start(f32[1,1024,512]{2,1,0:T(8,128)} %param.13) | copy-start | bytes 6291460
  3.8 111.3 %copy-start.5 = (f32[1,1024,512]{2,1,0:T(8,128)S(1)}, f32[1,1024,512]{2,1,0:T(8,128)}, u32[]{:S(2)}) copy-start(f32[1,1024,512]{2,1,0:T(8,128)} %param.12) | copy-start | bytes 6291460
  115.1 5.4 %copy-start.2 = (f32[1024,512]{1,0:T(8,128)S(1)}, f32[1024,512]{1,0:T(8,128)}, u32[]{:S(2)}) copy-start(f32[1024,512]{1,0:T(8,128)} %momentum.1) | copy-start | bytes 6291460

commit v2 on v1

--- a/solution.py
+++ b/solution.py
@@ -121,8 +121,147 @@
         part_copy(k).wait_send()
 
 
+HALVES = 2
+
+
+def line_kernel(
+    tokens, cot, grad, tok_p, cot_p, part, recv,
+    cot_send, cot_recv, tok_send, tok_recv, part_send, part_recv,
+):
+    rows = grad.shape[0]
+    half = rows // HALVES
+    tile = min(half, 256)
+    r, f = lax.axis_index("rep"), lax.axis_index("fsdp")
+    o, b = f // 2, f % 2
+    partner = 2 * o + 1 - b
+    side = o // 2
+    inner = (o + side) % 2
+
+    def pair(q):
+        return q + side * (3 - 2 * q)
+
+    greet(r, partner)
+    for k in range(1, 4):
+        greet(r, 2 * ((o + k) % 4) + b)
+    pl.semaphore_wait(pltpu.get_barrier_semaphore(), 4)
+
+    def block(i):
+        return (3 + inner - i) % 4
+
+    def cot_copy():
+        return remote(cot, cot_p, cot_send, cot_recv, r, partner)
+
+    def tok_copy(i, h):
+        col = pl.multiple_of((2 * pair(block(i)) + 1 - b) * rows + h * half, half)
+        return remote(
+            tokens.at[:, pl.ds(col, half)], tok_p.at[i, h],
+            tok_send.at[i, h], tok_recv.at[i, h], r, partner,
+        )
+
+    def part_copy(i, h):
+        slot = i + inner * (2, 2, 1)[i]
+        to = pair(inner * block(i) + 1 - inner)
+        return remote(
+            part.at[i, h], recv.at[slot, h], part_send.at[i, h], part_recv.at[slot, h],
+            r, 2 * to + b,
+        )
+
+    def received(slot, h):
+        return remote(
+            part.at[0, h], recv.at[slot, h], part_send.at[0, h], part_recv.at[slot, h],
+            r, partner,
+        )
+
+    def partial(i, h, j):
+        first = pl.multiple_of(j * tile, tile)
+        col = pl.multiple_of((2 * pair(block(i)) + b) * rows + h * half + first, tile)
+        return contract_rows(tokens[:, pl.ds(col, tile)], cot[...]) + contract_rows(
+            tok_p[i, h, :, pl.ds(first, tile)], cot_p[...]
+        )
+
+    cot_copy().start()
+    for i in range(4):
+        for h in range(HALVES):
+            tok_copy(i, h).start()
+    cot_copy().wait_recv()
+    for i in range(3):
+        for h in range(HALVES):
+            tok_copy(i, h).wait_recv()
+
+            @pl.when((inner == 0) | (i == 0))
+            def _():
+                @pl.loop(0, half // tile)
+                def _(j):
+                    at = pl.ds(pl.multiple_of(j * tile, tile), tile)
+                    part[i, h, at, :] = partial(i, h, j).astype(part.dtype)
+
+            if i > 0:
+                @pl.when(inner == 1)
+                def _():
+                    received(i - 1, h).wait_recv()
+
+                    @pl.loop(0, half // tile)
+                    def _(j):
+                        at = pl.ds(pl.multiple_of(j * tile, tile), tile)
+                        total = partial(i, h, j) + recv[i - 1, h, at, :].astype(jnp.float32)
+                        part[i, h, at, :] = total.astype(part.dtype)
+
+            part_copy(i, h).start()
+
+    for h in range(HALVES):
+        tok_copy(3, h).wait_recv()
+
+        @pl.loop(0, half // tile)
+        def _(j):
+            at = pl.ds(pl.multiple_of(h * half + j * tile, tile), tile)
+            grad[at, :] = partial(3, h, j)
+
+    for h in range(HALVES):
+        for slot in (2, 3):
+            received(slot, h).wait_recv()
+
+            @pl.loop(0, half // tile)
+            def _(j):
+                at = pl.ds(pl.multiple_of(h * half + j * tile, tile), tile)
+                there = pl.ds(pl.multiple_of(j * tile, tile), tile)
+                grad[at, :] += recv[slot, h, there, :].astype(jnp.float32)
+
+    cot_copy().wait_send()
+    for h in range(HALVES):
+        for i in range(4):
+            tok_copy(i, h).wait_send()
+        for i in range(3):
+            part_copy(i, h).wait_send()
+
+
+def line_grad(tokens, cotangent):
+    count, width = tokens.shape
+    kh = cotangent.shape[1]
+    rows = width // 8
+    half = rows // HALVES
+    dma = pltpu.SemaphoreType.DMA
+    return pl.pallas_call(
+        line_kernel,
+        out_shape=jax.ShapeDtypeStruct((rows, kh), jnp.float32),
+        in_specs=[VMEM] * 2,
+        out_specs=VMEM,
+        scratch_shapes=[
+            pltpu.VMEM((4, HALVES, count, half), jnp.bfloat16),
+            pltpu.VMEM((count, kh), jnp.bfloat16),
+            pltpu.VMEM((3, HALVES, half, kh), jnp.bfloat16),
+            pltpu.VMEM((4, HALVES, half, kh), jnp.bfloat16),
+            dma, dma, dma((4, HALVES)), dma((4, HALVES)), dma((3, HALVES)), dma((4, HALVES)),
+        ],
+        compiler_params=pltpu.CompilerParams(
+            collective_id=0, has_side_effects=True, vmem_limit_bytes=40 * 2**20
+        ),
+    )(tokens, cotangent)
+
+
 def group_grad(mesh, tokens, cotangent):
     n = mesh.shape["fsdp"]
+    if n == 8:
+        return line_grad(tokens, cotangent)
     outer = n // 2
     count, width = tokens.shape
     kh = cotangent.shape[1]

time: 201 us -> 173 us (0.86); the launches traced: 198 us -> 173 us
  Pallas kernels: 189 us -> 163 us
    pallas_call x1, Pallas kernels: 111 us -> 81 us  [line_grad(): pl.pallas_call(line_kernel, out_shape=jax.ShapeDtypeStruct((rows, kh), jn...]
    pallas_call x1, Pallas kernels: 77.3 us -> 82.2 us  [keys_of(): pl.pallas_call(functools.partial(keys_kernel, n), out_shape=jax.ShapeDtyp...]
where the time goes in v2:
time: 173 us
  Pallas kernels  163 us (94%)
  other arithmetic  5.35 us (3%)
  local copies, waits for them, and re-layouts  3.85 us (2%)
    pallas_call x1, Pallas kernels, keys_of(): pl.pallas_call(functools.partial(keys_kernel, n), out_shape=jax.ShapeDtyp...  82.2 us
    pallas_call x1, Pallas kernels, line_grad(): pl.pallas_call(line_kernel, out_shape=jax.ShapeDtypeStruct((rows, kh), jn...  81 us
    convert_element_type x1, other arithmetic, on_device(): delta = (anchor - inner[0]).astype(jnp.bfloat16)  5.35 us
    unnamed x13, local copies, waits for them, and re-layouts  3.85 us

profile of v2, /device:TPU:17, one launch (start us, length us, event | category | flops | bytes accessed | tf_op | source)
XLA Modules:
  0.0 173.0 jit_solution(247974272762854815)
XLA Ops:
  0.6 0.0 copy-start
  0.6 2.2 %copy-done = bf16[256,8192]{1,0:T(8,128)(2,1)S(1)} copy-done((bf16[256,8192]{1,0:T(8,128)(2,1)S(1)}, bf16[256,8192]{1,0:T(8,128)(2,1)}, u32[]{:S(2)}) %copy-start) | copy-done | bytes 4194328
  2.8 0.0 copy-start.3
  2.8 0.9 copy-done.3
  3.8 0.0 copy-start.1
  3.8 0.0 copy-start.4
  3.8 0.0 copy-start.5
  3.8 81.0 %shard_map.94 = f32[1024,512]{1,0:T(8,128)S(1)} custom-call(bf16[256,8192]{1,0:T(8,128)(2,1)S(1)} %copy-done, bf16[256,512]{1,0:T(8,128)(2,1)S(1)} %copy-done.3), custom_call_target="tpu_custom_call" | custom-call | tf_op jit(solution)/shard_map/pallas_call | solution.py:243
  84.7 0.0 copy-done.1
  84.7 0.0 copy-done.4
  84.8 0.0 copy-done.5
  84.8 0.0 copy-start.2
  84.8 5.3 %fusion.2 = (bf16[1024,512]{1,0:T(8,128)(2,1)S(1)}, f32[1,1024,512]{2,1,0:T(8,128)}, f32[1,1024,512]{2,1,0:T(8,128)}) fusion(f32[1024,512]{1,0:T(8,128)S(1)} %copy-done.1, f32[1,1024,512]{2,1,0:T(8,128)S(1)} %copy-done.4, f32[1024,512]{1,0:T(8,128)S(1)} %shard_map.94, f32[1,1024,512]{2,1,0:T(8,128)S(1)} %copy-done.5, f32[1,1024,512]{2,1,0:T(8,128)} %param.11), kind=kLoop, calls=%fused_computation.4 | loop fusion | flops 8388608 | bytes 15728640 | tf_op jit(solution)/shard_map/convert_element_type | solution.py:451
  90.1 0.0 copy-done.2
  90.1 82.2 %shard_map.95 = bf16[256,512]{1,0:T(8,128)(2,1)S(1)} custom-call(bf16[256,8192]{1,0:T(8,128)(2,1)S(1)} %copy-done, bf16[1024,512]{1,0:T(8,128)(2,1)S(1)} %get-tuple-element.3.delta, f32[1024,512]{1,0:T(8,128)S(1)} %copy-done.1, f32[1024,512]{1,0:T(8,128)S(1)} %copy-done.2), custom_call_target="tpu_custom_call" | custom-call | tf_op jit(solution)/shard_map/pallas_call | solution.py:425
  172.3 0.7 copy.11
Async XLA Ops:
  0.6 2.2 %copy-start = (bf16[256,8192]{1,0:T(8,128)(2,1)S(1)}, bf16[256,8192]{1,0:T(8,128)(2,1)}, u32[]{:S(2)}) copy-start(bf16[256,8192]{1,0:T(8,128)(2,1)} %tokens.3) | copy-start | bytes 12582916
  2.8 0.9 copy-start.3
  3.8 81.0 %copy-start.1 = (f32[1024,512]{1,0:T(8,128)S(1)}, f32[1024,512]{1,0:T(8,128)}, u32[]{:S(2)}) copy-start(f32[1024,512]{1,0:T(8,128)} %anchor.1) | copy-start | bytes 6291460
  3.8 81.0 %copy-start.4 = (f32[1,1024,512]{2,1,0:T(8,128)S(1)}, f32[1,1024,512]{2,1,0:T(8,128)}, u32[]{:S(2)}) copy-start(f32[1,1024,512]{2,1,0:T(8,128)} %param.13) | copy-start | bytes 6291460
  3.8 81.0 %copy-start.5 = (f32[1,1024,512]{2,1,0:T(8,128)S(1)}, f32[1,1024,512]{2,1,0:T(8,128)}, u32[]{:S(2)}) copy-start(f32[1,1024,512]{2,1,0:T(8,128)} %param.12) | copy-start | bytes 6291460
  84.8 5.4 %copy-start.2 = (f32[1024,512]{1,0:T(8,128)S(1)}, f32[1024,512]{1,0:T(8,128)}, u32[]{:S(2)}) copy-start(f32[1024,512]{1,0:T(8,128)} %momentum.1) | copy-start | bytes 6291460

commit v3 on v2

--- a/solution.py
+++ b/solution.py
@@ -287,8 +287,8 @@
 
 def keys_kernel(
     n, tokens, delta, anchor, momentum, keys, got, weights, total,
-    got_send, got_recv, z_send, z_recv, x_send, x_recv,
-    y_send, y_recv, c_send, c_recv, d_send, d_recv,
+    got_send, got_recv, z_send, z_recv, first_send, first_recv,
+    second_send, second_recv, near_send, near_recv,
 ):
     outer = n // 2
     rows = anchor.shape[0]
@@ -311,8 +311,9 @@
     def quarter_of(rep):
         return pl.ds(pl.multiple_of(rep * quarter, quarter), quarter)
 
-    def chunk(fsdp, rep):
-        return weights.at[pl.ds(pl.multiple_of(fsdp * rows + rep * quarter, quarter), quarter)]
+    def chunk(fsdp, rep, h):
+        at = fsdp * rows + rep * quarter + h * (quarter // 2)
+        return weights.at[pl.ds(pl.multiple_of(at, quarter // 2), quarter // 2)]
 
     def got_copy(m):
         to = (r + m) % 4
@@ -335,32 +336,40 @@
     own = pl.ds(pl.multiple_of(f * rows + r * quarter, quarter), quarter)
     weights[own, :] = anchor_new.astype(weights.dtype)
 
-    def z_copy(k):
-        ref = chunk(f, r)
-        return remote(ref, ref, z_send.at[k], z_recv.at[k], r, 2 * ((o + k) % outer) + b)
+    def z_copy(k, h):
+        ref = chunk(f, r, h)
+        return remote(ref, ref, z_send.at[k, h], z_recv.at[k, h], r, 2 * ((o + k) % outer) + b)
 
     def source(k, parity):
         return 2 * ((o + outer - k) % outer) + parity
 
-    def x_copy(k):
-        ref = chunk(source(k, b), r)
-        return remote(ref, ref, x_send.at[k], x_recv.at[k], r, partner)
-
-    def y_copy(k, s):
-        ref = chunk(source(k, b if s == 0 else 1 - b), r)
-        return remote(ref, ref, y_send.at[k, s], y_recv.at[k, s], over, f)
-
-    def c_copy(k, s):
-        ref = chunk(source(k, b if s == 0 else 1 - b), r)
-        return remote(ref, ref, c_send.at[k, s], c_recv.at[k, s], near, f)
-
-    def d_copy(k, s):
-        ref = chunk(source(k, b if s == 0 else 1 - b), over)
-        return remote(ref, ref, d_send.at[k, s], d_recv.at[k, s], near, f)
-
-    @pl.loop(1, outer)
-    def _(k):
-        z_copy(k).start()
+    def held(k, h, which):
+        first, second = which % 2, which // 2
+        flip, far = (first, second) if h == 0 else (second, first)
+        return chunk(source(k, 1 - b if flip else b), over if far else r, h)
+
+    def first_copy(k, h):
+        ref = held(k, h, 0)
+        to = (r, partner) if h == 0 else (over, f)
+        return remote(ref, ref, first_send.at[k, h], first_recv.at[k, h], *to)
+
+    def second_copy(k, h, which):
+        ref = held(k, h, which)
+        to = (over, f) if h == 0 else (r, partner)
+        return remote(
+            ref, ref, second_send.at[k, h, which], second_recv.at[k, h, which], *to
+        )
+
+    def near_copy(k, h, which):
+        ref = held(k, h, which)
+        return remote(
+            ref, ref, near_send.at[k, h, which], near_recv.at[k, h, which], near, f
+        )
+
+    @pl.loop(1, outer)
+    def _(k):
+        for h in range(2):
+            z_copy(k, h).start()
 
     total[...] = jnp.zeros_like(total)
 
@@ -368,32 +377,35 @@
     def _(i):
         @pl.when(i < outer)
         def _():
-            @pl.when(i > 0)
-            def _():
-                z_copy(i).wait_recv()
-
-            x_copy(i).start()
-            y_copy(i, 0).start()
-            c_copy(i, 0).start()
+            for h in range(2):
+                @pl.when(i > 0)
+                def _():
+                    z_copy(i, h).wait_recv()
+
+                first_copy(i, h).start()
+                second_copy(i, h, 0).start()
+                near_copy(i, h, 0).start()
 
         @pl.when((i >= 1) & (i < outer + 1))
         def _():
-            x_copy(i - 1).wait_recv()
-            y_copy(i - 1, 1).start()
-            c_copy(i - 1, 1).start()
+            for h in range(2):
+                first_copy(i - 1, h).wait_recv()
+                second_copy(i - 1, h, 1).start()
+                near_copy(i - 1, h, 1).start()
 
         @pl.when((i >= 2) & (i < outer + 2))
         def _():
-            for s in range(2):
-                y_copy(i - 2, s).wait_recv()
-                d_copy(i - 2, s).start()
+            for which in range(2):
+                for h in range(2):
+                    second_copy(i - 2, h, which).wait_recv()
+                    near_copy(i - 2, h, 2 + which).start()
 
         @pl.when(i >= 3)
         def _():
             k = i - 3
-            for s in range(2):
-                c_copy(k, s).wait_recv()
-                d_copy(k, s).wait_recv()
+            for h in range(2):
+                for which in range(4):
+                    near_copy(k, h, which).wait_recv()
             at = pl.ds(pl.multiple_of(source(k, 0) * rows, 2 * rows), 2 * rows)
             total[...] += jnp.dot(
                 tokens[:, at], weights[at, :], preferred_element_type=jnp.float32
@@ -405,15 +417,16 @@
 
     @pl.loop(0, outer)
     def _(k):
-        @pl.when(k > 0)
-        def _():
-            z_copy(k).wait_send()
-
-        x_copy(k).wait_send()
-        for s in range(2):
-            y_copy(k, s).wait_send()
-            c_copy(k, s).wait_send()
-            d_copy(k, s).wait_send()
+        for h in range(2):
+            @pl.when(k > 0)
+            def _():
+                z_copy(k, h).wait_send()
+
+            first_copy(k, h).wait_send()
+            for which in range(2):
+                second_copy(k, h, which).wait_send()
+            for which in range(4):
+                near_copy(k, h, which).wait_send()
 
 
 def keys_of(mesh, tokens, delta, anchor, momentum):
@@ -432,9 +445,8 @@
             pltpu.VMEM((width, kh), jnp.bfloat16),
             pltpu.VMEM((count, kh), jnp.float32),
             dma((3,)), dma((3,)),
-            dma((outer,)), dma((outer,)), dma((outer,)), dma((outer,)),
             dma((outer, 2)), dma((outer, 2)), dma((outer, 2)), dma((outer, 2)),
-            dma((outer, 2)), dma((outer, 2)),
+            dma((outer, 2, 2)), dma((outer, 2, 2)), dma((outer, 2, 4)), dma((outer, 2, 4)),
         ],
         compiler_params=pltpu.CompilerParams(
             collective_id=1, has_side_effects=True, vmem_limit_bytes=40 * 2**20

time: 173 us -> 160 us (0.925)
  Pallas kernels: 163 us -> 150 us
    pallas_call x1, Pallas kernels: 82.2 us -> 68.8 us  [keys_of(): pl.pallas_call(functools.partial(keys_kernel, n), out_shape=jax.ShapeDtyp...]
where the time goes in v3:
time: 160 us
  Pallas kernels  150 us (94%)
  other arithmetic  5.35 us (3%)
  local copies, waits for them, and re-layouts  3.85 us (2%)
    pallas_call x1, Pallas kernels, line_grad(): pl.pallas_call(line_kernel, out_shape=jax.ShapeDtypeStruct((rows, kh), jn...  81 us
    pallas_call x1, Pallas kernels, keys_of(): pl.pallas_call(functools.partial(keys_kernel, n), out_shape=jax.ShapeDtyp...  68.8 us
    convert_element_type x1, other arithmetic, on_device(): delta = (anchor - inner[0]).astype(jnp.bfloat16)  5.35 us
    unnamed x13, local copies, waits for them, and re-layouts  3.85 us

profile of v3, /device:TPU:17, one launch (start us, length us, event | category | flops | bytes accessed | tf_op | source)
XLA Modules:
  0.0 159.6 jit_solution(6901858876343611918)
XLA Ops:
  0.6 0.0 copy-start
  0.6 2.2 %copy-done = bf16[256,8192]{1,0:T(8,128)(2,1)S(1)} copy-done((bf16[256,8192]{1,0:T(8,128)(2,1)S(1)}, bf16[256,8192]{1,0:T(8,128)(2,1)}, u32[]{:S(2)}) %copy-start) | copy-done | bytes 4194328
  2.8 0.0 copy-start.3
  2.8 0.9 copy-done.3
  3.8 0.0 copy-start.1
  3.8 0.0 copy-start.4
  3.8 0.0 copy-start.5
  3.8 81.0 %shard_map.94 = f32[1024,512]{1,0:T(8,128)S(1)} custom-call(bf16[256,8192]{1,0:T(8,128)(2,1)S(1)} %copy-done, bf16[256,512]{1,0:T(8,128)(2,1)S(1)} %copy-done.3), custom_call_target="tpu_custom_call" | custom-call | tf_op jit(solution)/shard_map/pallas_call | solution.py:243
  84.7 0.0 copy-done.1
  84.7 0.0 copy-done.4
  84.8 0.0 copy-done.5
  84.8 0.0 copy-start.2
  84.8 5.3 %fusion.2 = (bf16[1024,512]{1,0:T(8,128)(2,1)S(1)}, f32[1,1024,512]{2,1,0:T(8,128)}, f32[1,1024,512]{2,1,0:T(8,128)}) fusion(f32[1024,512]{1,0:T(8,128)S(1)} %copy-done.1, f32[1,1024,512]{2,1,0:T(8,128)S(1)} %copy-done.4, f32[1024,512]{1,0:T(8,128)S(1)} %shard_map.94, f32[1,1024,512]{2,1,0:T(8,128)S(1)} %copy-done.5, f32[1,1024,512]{2,1,0:T(8,128)} %param.11), kind=kLoop, calls=%fused_computation.4 | loop fusion | flops 8388608 | bytes 15728640 | tf_op jit(solution)/shard_map/convert_element_type | solution.py:463
  90.1 0.0 copy-done.2
  90.1 68.8 %shard_map.95 = bf16[256,512]{1,0:T(8,128)(2,1)S(1)} custom-call(bf16[256,8192]{1,0:T(8,128)(2,1)S(1)} %copy-done, bf16[1024,512]{1,0:T(8,128)(2,1)S(1)} %get-tuple-element.3.delta, f32[1024,512]{1,0:T(8,128)S(1)} %copy-done.1, f32[1024,512]{1,0:T(8,128)S(1)} %copy-done.2), custom_call_target="tpu_custom_call" | custom-call | tf_op jit(solution)/shard_map/pallas_call | solution.py:438
  158.9 0.7 copy.11
Async XLA Ops:
  0.6 2.2 %copy-start = (bf16[256,8192]{1,0:T(8,128)(2,1)S(1)}, bf16[256,8192]{1,0:T(8,128)(2,1)}, u32[]{:S(2)}) copy-start(bf16[256,8192]{1,0:T(8,128)(2,1)} %tokens.3) | copy-start | bytes 12582916
  2.8 0.9 copy-start.3
  3.8 81.0 %copy-start.1 = (f32[1024,512]{1,0:T(8,128)S(1)}, f32[1024,512]{1,0:T(8,128)}, u32[]{:S(2)}) copy-start(f32[1024,512]{1,0:T(8,128)} %anchor.1) | copy-start | bytes 6291460
  3.8 81.0 %copy-start.4 = (f32[1,1024,512]{2,1,0:T(8,128)S(1)}, f32[1,1024,512]{2,1,0:T(8,128)}, u32[]{:S(2)}) copy-start(f32[1,1024,512]{2,1,0:T(8,128)} %param.13) | copy-start | bytes 6291460
  3.8 81.0 %copy-start.5 = (f32[1,1024,512]{2,1,0:T(8,128)S(1)}, f32[1,1024,512]{2,1,0:T(8,128)}, u32[]{:S(2)}) copy-start(f32[1,1024,512]{2,1,0:T(8,128)} %param.12) | copy-start | bytes 6291460
  84.8 5.4 %copy-start.2 = (f32[1024,512]{1,0:T(8,128)S(1)}, f32[1024,512]{1,0:T(8,128)}, u32[]{:S(2)}) copy-start(f32[1024,512]{1,0:T(8,128)} %momentum.1) | copy-start | bytes 6291460

commit v4 on v3

--- a/solution.py
+++ b/solution.py
@@ -121,7 +121,7 @@
         part_copy(k).wait_send()
 
 
-HALVES = 2
+PIECES = 4
 
 
 def line_kernel(
@@ -129,8 +129,8 @@
     cot_send, cot_recv, tok_send, tok_recv, part_send, part_recv,
 ):
     rows = grad.shape[0]
-    half = rows // HALVES
-    tile = min(half, 256)
+    size = rows // PIECES
+    tile = min(size, 256)
     r, f = lax.axis_index("rep"), lax.axis_index("fsdp")
     o, b = f // 2, f % 2
     partner = 2 * o + 1 - b
@@ -152,9 +152,9 @@
         return remote(cot, cot_p, cot_send, cot_recv, r, partner)
 
     def tok_copy(i, h):
-        col = pl.multiple_of((2 * pair(block(i)) + 1 - b) * rows + h * half, half)
-        return remote(
-            tokens.at[:, pl.ds(col, half)], tok_p.at[i, h],
+        col = pl.multiple_of((2 * pair(block(i)) + 1 - b) * rows + h * size, size)
+        return remote(
+            tokens.at[:, pl.ds(col, size)], tok_p.at[i, h],
             tok_send.at[i, h], tok_recv.at[i, h], r, partner,
         )
 
@@ -174,23 +174,23 @@
 
     def partial(i, h, j):
         first = pl.multiple_of(j * tile, tile)
-        col = pl.multiple_of((2 * pair(block(i)) + b) * rows + h * half + first, tile)
+        col = pl.multiple_of((2 * pair(block(i)) + b) * rows + h * size + first, tile)
         return contract_rows(tokens[:, pl.ds(col, tile)], cot[...]) + contract_rows(
             tok_p[i, h, :, pl.ds(first, tile)], cot_p[...]
         )
 
     cot_copy().start()
     for i in range(4):
-        for h in range(HALVES):
+        for h in range(PIECES):
             tok_copy(i, h).start()
     cot_copy().wait_recv()
     for i in range(3):
-        for h in range(HALVES):
+        for h in range(PIECES):
             tok_copy(i, h).wait_recv()
 
             @pl.when((inner == 0) | (i == 0))
             def _():
-                @pl.loop(0, half // tile)
+                @pl.loop(0, size // tile)
                 def _(j):
                     at = pl.ds(pl.multiple_of(j * tile, tile), tile)
                     part[i, h, at, :] = partial(i, h, j).astype(part.dtype)
@@ -200,7 +200,7 @@
                 def _():
                     received(i - 1, h).wait_recv()
 
-                    @pl.loop(0, half // tile)
+                    @pl.loop(0, size // tile)
                     def _(j):
                         at = pl.ds(pl.multiple_of(j * tile, tile), tile)
                         total = partial(i, h, j) + recv[i - 1, h, at, :].astype(jnp.float32)
@@ -208,26 +208,26 @@
 
             part_copy(i, h).start()
 
-    for h in range(HALVES):
+    for h in range(PIECES):
         tok_copy(3, h).wait_recv()
 
-        @pl.loop(0, half // tile)
+        @pl.loop(0, size // tile)
         def _(j):
-            at = pl.ds(pl.multiple_of(h * half + j * tile, tile), tile)
+            at = pl.ds(pl.multiple_of(h * size + j * tile, tile), tile)
             grad[at, :] = partial(3, h, j)
 
-    for h in range(HALVES):
+    for h in range(PIECES):
         for slot in (2, 3):
             received(slot, h).wait_recv()
 
-            @pl.loop(0, half // tile)
+            @pl.loop(0, size // tile)
             def _(j):
-                at = pl.ds(pl.multiple_of(h * half + j * tile, tile), tile)
+                at = pl.ds(pl.multiple_of(h * size + j * tile, tile), tile)
                 there = pl.ds(pl.multiple_of(j * tile, tile), tile)
                 grad[at, :] += recv[slot, h, there, :].astype(jnp.float32)
 
     cot_copy().wait_send()
-    for h in range(HALVES):
+    for h in range(PIECES):
         for i in range(4):
             tok_copy(i, h).wait_send()
         for i in range(3):
@@ -238,7 +238,7 @@
     count, width = tokens.shape
     kh = cotangent.shape[1]
     rows = width // 8
-    half = rows // HALVES
+    size = rows // PIECES
     dma = pltpu.SemaphoreType.DMA
     return pl.pallas_call(
         line_kernel,
@@ -246,11 +246,11 @@
         in_specs=[VMEM] * 2,
         out_specs=VMEM,
         scratch_shapes=[
-            pltpu.VMEM((4, HALVES, count, half), jnp.bfloat16),
+            pltpu.VMEM((4, PIECES, count, size), jnp.bfloat16),
             pltpu.VMEM((count, kh), jnp.bfloat16),
-            pltpu.VMEM((3, HALVES, half, kh), jnp.bfloat16),
-            pltpu.VMEM((4, HALVES, half, kh), jnp.bfloat16),
-            dma, dma, dma((4, HALVES)), dma((4, HALVES)), dma((3, HALVES)), dma((4, HALVES)),
+            pltpu.VMEM((3, PIECES, size, kh), jnp.bfloat16),
+            pltpu.VMEM((4, PIECES, size, kh), jnp.bfloat16),
+            dma, dma, dma((4, PIECES)), dma((4, PIECES)), dma((3, PIECES)), dma((4, PIECES)),
         ],
         compiler_params=pltpu.CompilerParams(
             collective_id=0, has_side_effects=True, vmem_limit_bytes=40 * 2**20

time: 160 us -> 157 us (0.981)
  Pallas kernels: 150 us -> 147 us
    pallas_call x1, Pallas kernels: 81 us -> 78.1 us  [line_grad(): pl.pallas_call(line_kernel, out_shape=jax.ShapeDtypeStruct((rows, kh), jn...]
where the time goes in v4:
time: 157 us
  Pallas kernels  147 us (94%)
  other arithmetic  5.35 us (3%)
  local copies, waits for them, and re-layouts  3.85 us (2%)
    pallas_call x1, Pallas kernels, line_grad(): pl.pallas_call(line_kernel, out_shape=jax.ShapeDtypeStruct((rows, kh), jn...  78.1 us
    pallas_call x1, Pallas kernels, keys_of(): pl.pallas_call(functools.partial(keys_kernel, n), out_shape=jax.ShapeDtyp...  68.7 us
    convert_element_type x1, other arithmetic, on_device(): delta = (anchor - inner[0]).astype(jnp.bfloat16)  5.35 us
    unnamed x13, local copies, waits for them, and re-layouts  3.85 us

profile of v4, /device:TPU:17, one launch (start us, length us, event | category | flops | bytes accessed | tf_op | source)
XLA Modules:
  0.0 156.7 jit_solution(345420110094408077)
XLA Ops:
  0.6 0.0 copy-start
  0.6 2.2 %copy-done = bf16[256,8192]{1,0:T(8,128)(2,1)S(1)} copy-done((bf16[256,8192]{1,0:T(8,128)(2,1)S(1)}, bf16[256,8192]{1,0:T(8,128)(2,1)}, u32[]{:S(2)}) %copy-start) | copy-done | bytes 4194328
  2.8 0.0 copy-start.3
  2.8 0.9 copy-done.3
  3.8 0.0 copy-start.1
  3.8 0.0 copy-start.4
  3.8 0.0 copy-start.5
  3.8 78.1 %shard_map.94 = f32[1024,512]{1,0:T(8,128)S(1)} custom-call(bf16[256,8192]{1,0:T(8,128)(2,1)S(1)} %copy-done, bf16[256,512]{1,0:T(8,128)(2,1)S(1)} %copy-done.3), custom_call_target="tpu_custom_call" | custom-call | tf_op jit(solution)/shard_map/pallas_call | solution.py:243
  81.9 0.0 copy-done.1
  81.9 0.0 copy-done.4
  81.9 0.0 copy-done.5
  81.9 0.0 copy-start.2
  81.9 5.3 %fusion.2 = (bf16[1024,512]{1,0:T(8,128)(2,1)S(1)}, f32[1,1024,512]{2,1,0:T(8,128)}, f32[1,1024,512]{2,1,0:T(8,128)}) fusion(f32[1024,512]{1,0:T(8,128)S(1)} %copy-done.1, f32[1,1024,512]{2,1,0:T(8,128)S(1)} %copy-done.4, f32[1024,512]{1,0:T(8,128)S(1)} %shard_map.94, f32[1,1024,512]{2,1,0:T(8,128)S(1)} %copy-done.5, f32[1,1024,512]{2,1,0:T(8,128)} %param.11), kind=kLoop, calls=%fused_computation.4 | loop fusion | flops 8388608 | bytes 15728640 | tf_op jit(solution)/shard_map/convert_element_type | solution.py:463
  87.2 0.0 copy-done.2
  87.3 68.7 %shard_map.95 = bf16[256,512]{1,0:T(8,128)(2,1)S(1)} custom-call(bf16[256,8192]{1,0:T(8,128)(2,1)S(1)} %copy-done, bf16[1024,512]{1,0:T(8,128)(2,1)S(1)} %get-tuple-element.3.delta, f32[1024,512]{1,0:T(8,128)S(1)} %copy-done.1, f32[1024,512]{1,0:T(8,128)S(1)} %copy-done.2), custom_call_target="tpu_custom_call" | custom-call | tf_op jit(solution)/shard_map/pallas_call | solution.py:438
  156.0 0.7 copy.11
Async XLA Ops:
  0.6 2.2 %copy-start = (bf16[256,8192]{1,0:T(8,128)(2,1)S(1)}, bf16[256,8192]{1,0:T(8,128)(2,1)}, u32[]{:S(2)}) copy-start(bf16[256,8192]{1,0:T(8,128)(2,1)} %tokens.3) | copy-start | bytes 12582916
  2.8 0.9 copy-start.3
  3.8 78.1 %copy-start.1 = (f32[1024,512]{1,0:T(8,128)S(1)}, f32[1024,512]{1,0:T(8,128)}, u32[]{:S(2)}) copy-start(f32[1024,512]{1,0:T(8,128)} %anchor.1) | copy-start | bytes 6291460
  3.8 78.1 %copy-start.4 = (f32[1,1024,512]{2,1,0:T(8,128)S(1)}, f32[1,1024,512]{2,1,0:T(8,128)}, u32[]{:S(2)}) copy-start(f32[1,1024,512]{2,1,0:T(8,128)} %param.13) | copy-start | bytes 6291460
  3.8 78.1 %copy-start.5 = (f32[1,1024,512]{2,1,0:T(8,128)S(1)}, f32[1,1024,512]{2,1,0:T(8,128)}, u32[]{:S(2)}) copy-start(f32[1,1024,512]{2,1,0:T(8,128)} %param.12) | copy-start | bytes 6291460
  81.9 5.4 %copy-start.2 = (f32[1024,512]{1,0:T(8,128)S(1)}, f32[1024,512]{1,0:T(8,128)}, u32[]{:S(2)}) copy-start(f32[1024,512]{1,0:T(8,128)} %momentum.1) | copy-start | bytes 6291460

commit v5 on v4

--- a/solution.py
+++ b/solution.py
@@ -121,7 +121,7 @@
         part_copy(k).wait_send()
 
 
-PIECES = 4
+PIECES = 8
 
 
 def line_kernel(

time: 157 us -> 156 us (level)
  no operation moved by 1% of the time
where the time goes in v5:
time: 156 us
  Pallas kernels  146 us (94%)
  other arithmetic  5.35 us (3%)
  local copies, waits for them, and re-layouts  3.85 us (2%)
    pallas_call x1, Pallas kernels, line_grad(): pl.pallas_call(line_kernel, out_shape=jax.ShapeDtypeStruct((rows, kh), jn...  77.1 us
    pallas_call x1, Pallas kernels, keys_of(): pl.pallas_call(functools.partial(keys_kernel, n), out_shape=jax.ShapeDtyp...  68.8 us
    convert_element_type x1, other arithmetic, on_device(): delta = (anchor - inner[0]).astype(jnp.bfloat16)  5.35 us
    unnamed x13, local copies, waits for them, and re-layouts  3.85 us

profile of v5, /device:TPU:17, one launch (start us, length us, event | category | flops | bytes accessed | tf_op | source)
XLA Modules:
  0.0 155.7 jit_solution(16698958131855790248)
XLA Ops:
  0.6 0.0 copy-start
  0.6 2.2 %copy-done = bf16[256,8192]{1,0:T(8,128)(2,1)S(1)} copy-done((bf16[256,8192]{1,0:T(8,128)(2,1)S(1)}, bf16[256,8192]{1,0:T(8,128)(2,1)}, u32[]{:S(2)}) %copy-start) | copy-done | bytes 4194328
  2.8 0.0 copy-start.3
  2.8 0.9 copy-done.3
  3.8 0.0 copy-start.1
  3.8 0.0 copy-start.4
  3.8 0.0 copy-start.5
  3.8 77.1 %shard_map.94 = f32[1024,512]{1,0:T(8,128)S(1)} custom-call(bf16[256,8192]{1,0:T(8,128)(2,1)S(1)} %copy-done, bf16[256,512]{1,0:T(8,128)(2,1)S(1)} %copy-done.3), custom_call_target="tpu_custom_call" | custom-call | tf_op jit(solution)/shard_map/pallas_call | solution.py:243
  80.9 0.0 copy-done.1
  80.9 0.0 copy-done.4
  80.9 0.0 copy-done.5
  80.9 0.0 copy-start.2
  80.9 5.3 %fusion.2 = (bf16[1024,512]{1,0:T(8,128)(2,1)S(1)}, f32[1,1024,512]{2,1,0:T(8,128)}, f32[1,1024,512]{2,1,0:T(8,128)}) fusion(f32[1024,512]{1,0:T(8,128)S(1)} %copy-done.1, f32[1,1024,512]{2,1,0:T(8,128)S(1)} %copy-done.4, f32[1024,512]{1,0:T(8,128)S(1)} %shard_map.94, f32[1,1024,512]{2,1,0:T(8,128)S(1)} %copy-done.5, f32[1,1024,512]{2,1,0:T(8,128)} %param.11), kind=kLoop, calls=%fused_computation.4 | loop fusion | flops 8388608 | bytes 15728640 | tf_op jit(solution)/shard_map/convert_element_type | solution.py:463
  86.3 0.0 copy-done.2
  86.3 68.8 %shard_map.95 = bf16[256,512]{1,0:T(8,128)(2,1)S(1)} custom-call(bf16[256,8192]{1,0:T(8,128)(2,1)S(1)} %copy-done, bf16[1024,512]{1,0:T(8,128)(2,1)S(1)} %get-tuple-element.3.delta, f32[1024,512]{1,0:T(8,128)S(1)} %copy-done.1, f32[1024,512]{1,0:T(8,128)S(1)} %copy-done.2), custom_call_target="tpu_custom_call" | custom-call | tf_op jit(solution)/shard_map/pallas_call | solution.py:438
  155.0 0.7 copy.11
Async XLA Ops:
  0.6 2.2 %copy-start = (bf16[256,8192]{1,0:T(8,128)(2,1)S(1)}, bf16[256,8192]{1,0:T(8,128)(2,1)}, u32[]{:S(2)}) copy-start(bf16[256,8192]{1,0:T(8,128)(2,1)} %tokens.3) | copy-start | bytes 12582916
  2.8 0.9 copy-start.3
  3.8 77.1 %copy-start.1 = (f32[1024,512]{1,0:T(8,128)S(1)}, f32[1024,512]{1,0:T(8,128)}, u32[]{:S(2)}) copy-start(f32[1024,512]{1,0:T(8,128)} %anchor.1) | copy-start | bytes 6291460
  3.8 77.1 %copy-start.4 = (f32[1,1024,512]{2,1,0:T(8,128)S(1)}, f32[1,1024,512]{2,1,0:T(8,128)}, u32[]{:S(2)}) copy-start(f32[1,1024,512]{2,1,0:T(8,128)} %param.13) | copy-start | bytes 6291460
  3.8 77.1 %copy-start.5 = (f32[1,1024,512]{2,1,0:T(8,128)S(1)}, f32[1,1024,512]{2,1,0:T(8,128)}, u32[]{:S(2)}) copy-start(f32[1,1024,512]{2,1,0:T(8,128)} %param.12) | copy-start | bytes 6291460
  80.9 5.4 %copy-start.2 = (f32[1024,512]{1,0:T(8,128)S(1)}, f32[1024,512]{1,0:T(8,128)}, u32[]{:S(2)}) copy-start(f32[1024,512]{1,0:T(8,128)} %momentum.1) | copy-start | bytes 6291460
